TPU v7x, 32 devices: a whole 2x2x4 slice. The times are simulated.
32 devices in a mesh: groups: 2 (over x), factor: 16 (over z, y, core).
Axes of the slice: x: 2, y: 2, z: 4, core: 2. Of those that a mesh axis runs over, the one named last changes fastest.
Arguments:
- history: bfloat16 [640, 32768], P(None, 'factor'), may hold values from -6 to 6
- scenario_ids: int32 [2048], P('groups'), parts along dimension 0, may hold values from 0 to 639
- desk_ids: int32 [4096], P(('groups', 'factor')), parts along dimension 0, may hold values from 0 to 15, as said below
- column_ids: int32 [4096], P(('groups', 'factor')), parts along dimension 0, may hold values from 0 to 15
- live_count: int32 [32], P(('groups', 'factor')), parts along dimension 0, may hold values from 16 to 128, as said below
- delta_blocks: bfloat16 [4096, 128, 128], P(('groups', 'factor')), parts along dimension 0, may hold values from -0.078125 to 0.078125
- gamma_blocks: bfloat16 [4096, 128, 128], P(('groups', 'factor')), parts along dimension 0, may hold values from -0.078125 to 0.078125
Outputs:
- pnl: float32 [4096, 1024], P(('groups', 'factor')), parts along dimension 0
- book_total: float32 [2048], P('groups'), parts along dimension 0
There are 2 independent parts, one for each index of `groups`. A program takes and returns all parts, laid end to end along the dimension named above; an argument that names none is the same for every part. Nothing has to cross between parts.
Inputs may be any that keep to these rules, and one draw needn't show every extreme that they name: `desk_ids`: the desk of a slot held by index p of factor is (p + o) mod 16 for some o from -4 to 4. `live_count`: one index of factor holds exactly 128 live slots; slots at or past the count are ignored.
All inputs are finite; a program needn't handle non-finite values.
Results may differ from a plain program's by a relative error of at most 0.002.
Values sent between devices are 32-bit elements; how exact they have to be, the bound alone decides.
A program may use at most 64 MiB of HBM per device.

v0:
```python
import math

import jax
import jax.numpy as jnp
from jax import lax
from jax.sharding import PartitionSpec as P

REACH = 4


def passed_along(block, axis, distance):
    devices = range(lax.axis_size(axis))
    route = [((i - distance) % len(devices), i) for i in devices]
    return lax.ppermute(block, axis, route)


def per_device(history, scenario_ids, desk_ids, column_ids, live_count, delta_blocks, gamma_blocks):
    shocks = jnp.take(history, scenario_ids, axis=0)
    half_square = (0.5 * jnp.square(shocks.astype(jnp.float32))).astype(jnp.bfloat16)
    width = delta_blocks.shape[2]
    desk_rows = delta_blocks.shape[1]
    scenarios = scenario_ids.shape[0]
    shard_blocks = history.shape[1] // width
    shock_tiles = shocks.reshape(scenarios, shard_blocks, width)
    square_tiles = half_square.reshape(scenarios, shard_blocks, width)
    devices = lax.axis_size("factor")
    position = lax.axis_index("factor")
    span = 2 * REACH + 1
    live_total = live_count[0]
    tile_ids = (desk_ids - position + REACH + devices) % devices
    dims = (((1,), (1,)), ((), ()))

    def block_term(slot):
        column = column_ids[slot]
        shock_part = lax.dynamic_index_in_dim(shock_tiles, column, 1, keepdims=False)
        square_part = lax.dynamic_index_in_dim(square_tiles, column, 1, keepdims=False)
        delta_part = lax.dynamic_index_in_dim(delta_blocks, slot, 0, keepdims=False)
        gamma_part = lax.dynamic_index_in_dim(gamma_blocks, slot, 0, keepdims=False)
        result = lax.dot_general(delta_part, shock_part, dims, preferred_element_type=jnp.float32)
        return result + lax.dot_general(
            gamma_part, square_part, dims, preferred_element_type=jnp.float32
        )

    def add_block(slot, running):
        offset = tile_ids[slot] * desk_rows
        current = lax.dynamic_slice_in_dim(running, offset, desk_rows, 0)
        return lax.dynamic_update_slice_in_dim(running, current + block_term(slot), offset, 0)

    partial_value = lax.fori_loop(
        0, live_total, add_block, jnp.zeros((span * desk_rows, scenarios), jnp.float32)
    )
    tiles = partial_value.reshape(span, desk_rows, scenarios)
    moving = tiles[2 * REACH]
    for step_number in range(2 * REACH):
        moving = passed_along(moving, "factor", 1)
        moving = moving + tiles[2 * REACH - 1 - step_number]
    pnl = passed_along(moving, "factor", -REACH)
    root_groups = math.sqrt(devices * desk_rows)
    book_total = lax.psum(jnp.sum(pnl, axis=0), "factor") / root_groups
    return (pnl, book_total)


def solution(mesh):
    return jax.shard_map(
        per_device,
        mesh=mesh,
        in_specs=(
            P(None, "factor"),
            P("groups"),
            P(("groups", "factor")),
            P(("groups", "factor")),
            P(("groups", "factor")),
            P(("groups", "factor"), None, None),
            P(("groups", "factor"), None, None),
        ),
        out_specs=(P(("groups", "factor"), None), P("groups")),
        check_vma=False,
    )
```

profile of v0, /device:TPU:3, one launch (start us, length us, event | category | flops | bytes accessed | tf_op | source)
XLA Modules:
  0.0 1148.3 jit_solution(4885057710560283064)
XLA Ops:
  2.9 6.0 gather_fusion
  8.9 6.2 multiply_convert_fusion
  15.1 2.7 broadcast_in_dim.15
  17.8 353.7 %while.10 = (s32[]{:T(128)}, f32[1152,1024]{1,0:T(8,128)}, s32[]{:T(128)}, s32[128]{0:T(128)S(1)}, bf16[128,128,128]{2,1,0:T(8,128)(2,1)}, /*index=5*/s32[128]{0...) while((s32[]{:T(128)}, f32[1152,1024]{1,0:T(8,128)}, ...), condition=%wide.region_1.2_spmd, body=%wide.region_0.1_spmd.sunk | while | flops 67371024 | bytes 2687283 | solution.py:49
  31.3 2.2 fusion.27
  62.7 2.2 fusion.27
  78.4 2.2 fusion.27
  94.1 2.2 fusion.27
  109.8 2.2 fusion.27
  133.3 2.2 fusion.27
  141.1 2.2 fusion.27
  164.7 2.2 fusion.27
  172.5 2.2 fusion.27
  180.4 2.2 fusion.27
  188.2 2.2 fusion.27
  196.1 2.2 fusion.27
  203.9 2.2 fusion.27
  227.5 2.2 fusion.27
  251.0 2.2 fusion.27
  258.8 2.2 fusion.27
  274.5 2.2 fusion.27
  298.0 2.2 fusion.27
  305.9 2.2 fusion.27
  321.6 2.2 fusion.27
  329.4 2.2 fusion.27
  337.3 2.2 fusion.27
  345.1 2.2 fusion.27
  353.0 2.2 fusion.27
  360.8 2.2 fusion.27
  368.7 2.2 fusion.27
  372.8 653.0 %collective-permute-start = (f32[128,1024]{1,0:T(8,128)S(1)}, f32[128,1024]{1,0:T(8,128)S(1)}, u32[]{:S(2)}, u32[]{:S(2)}) collective-permute-start(f32[128,1024]{1,0:T(8,128)S(1)} %slice.36), channel_id=1, source_target_pairs={{15,0},{0,1},{1,2},{2,3},{3,4},{4,5},{5,6},{6,7},{7,8},{8,9},{9,10... | collective-permute-start | bytes 1572872 | tf_op jit(solution)/shard_map/ppermute | solution.py:14
  1025.8 6.1 collective-permute-done
  1033.0 2.5 collective-permute-start.1
  1035.6 6.1 collective-permute-done.1
  1042.8 2.5 collective-permute-start.2
  1045.3 6.1 collective-permute-done.2
  1052.6 2.5 collective-permute-start.3
  1055.1 6.1 collective-permute-done.3
  1061.3 2.5 collective-permute-start.4
  1063.8 6.1 collective-permute-done.4
  1070.0 2.5 collective-permute-start.5
  1072.6 6.1 collective-permute-done.5
  1078.8 2.5 collective-permute-start.6
  1081.3 6.1 collective-permute-done.6
  1087.5 2.5 collective-permute-start.7
  1090.0 6.1 collective-permute-done.7
  1096.3 8.3 collective-permute-done.8
  1104.6 42.3 %psum.7 = f32[1024]{0:T(1024)S(1)} all-reduce(f32[1024]{0:T(1024)S(1)} %reduce_sum.9), channel_id=1, replica_groups=mesh['groups'=2,'factor'=16] {'factor'}, use_global_device_ids=true, to_apply=%region_3.4 | all-reduce | flops 1024 | bytes 8192 | tf_op jit(solution)/shard_map/psum | solution.py:59
  (176 shorter events, 157.0 us)
Async XLA Ops:
  0.6 2.2 copy-start
  15.1 2.7 copy-start.2
  371.5 689.7 %copy-start.1 = (f32[1152,1024]{1,0:T(8,128)S(1)}, f32[1152,1024]{1,0:T(8,128)}, u32[]{:S(2)}) copy-start(f32[1152,1024]{1,0:T(8,128)} %get-tuple-element.50) | copy-start | bytes 14155780
  372.8 659.1 %collective-permute-start = (f32[128,1024]{1,0:T(8,128)S(1)}, f32[128,1024]{1,0:T(8,128)S(1)}, u32[]{:S(2)}, u32[]{:S(2)}) collective-permute-start(f32[128,1024]{1,0:T(8,128)S(1)} %slice.36), channel_id=1, source_target_pairs={{15,0},{0,1},{1,2},{2,3},{3,4},{4,5},{5,6},{6,7},{7,8},{8,9},{9,10... | collective-permute-start | bytes 1572872 | tf_op jit(solution)/shard_map/ppermute | solution.py:14
  1033.0 8.7 collective-permute-start.1
  1042.8 8.7 collective-permute-start.2
  1052.6 8.7 collective-permute-start.3
  1061.3 8.7 collective-permute-start.4
  1070.0 8.7 collective-permute-start.5
  1078.8 8.7 collective-permute-start.6
  1087.5 8.7 collective-permute-start.7
  1096.2 8.4 collective-permute-start.8
where the time goes:
time: 1170 us; the launch traced here: 1150 us
  starting transfers between devices  671 us (57%)
  matrix products  153 us (13%)
  loops' own time  148 us (13%)
  local copies, waits for them, and re-layouts  63.7 us (5%)
  waiting for transfers between devices  57.3 us (5%)
  blocking collectives  42.3 us (4%)
  other arithmetic  12.7 us (1%)
    ppermute x9, starting transfers between devices, passed_along(): return lax.ppermute(block, axis, route)  671 us
    another operation x1, loops' own time, per_device(): lax.fori_loop(0, live_total, add_block, jnp.zeros((span * desk_rows, scen...  148 us
    dot_general x45, matrix products, block_term(): lax.dot_general(gamma_part, square_part, dims, preferred_element_type=jnp...  98.7 us
    ppermute x9, waiting for transfers between devices, passed_along(): return lax.ppermute(block, axis, route)  57.3 us
    dot_general x45, matrix products, block_term(): lax.dot_general(delta_part, shock_part, dims, preferred_element_type=jnp....  54 us
    psum x1, blocking collectives, per_device(): book_total = lax.psum(jnp.sum(pnl, axis=0), 'factor') / root_groups  42.3 us
    dynamic_slice x45, local copies, waits for them, and re-layouts, block_term(): column = column_ids[slot]  26.5 us
    dynamic_slice x45, local copies, waits for them, and re-layouts, add_block(): offset = tile_ids[slot] * desk_rows  26.4 us
  transfers between devices with their start and end apart: 9, of which 9 were waited for; matrix products, arithmetic and copies ran while one was open for 0% of the time, Pallas kernels for 0%

commit v1 on v0

v1 whole, which is shorter than its diff:
```python
import functools
import math

import jax
import jax.numpy as jnp
from jax import lax
from jax.experimental import pallas as pl
from jax.experimental.pallas import tpu as pltpu
from jax.sharding import PartitionSpec as P

REACH = 4
SPAN = 2 * REACH + 1
CHUNK = 8
MIB = 1 << 20


def block_kernel(devices, desks, columns, live, hist_ref, delta_ref, gamma_ref, tiles_ref, days):
    step = pl.program_id(0)
    position = lax.axis_index("factor")
    chunk, _, width = delta_ref.shape

    @pl.when(step == 0)
    def _():
        tiles_ref[...] = jnp.zeros_like(tiles_ref)
        for c in range(days.shape[0]):
            shock = hist_ref[:, c * width:(c + 1) * width]
            wide = shock.astype(jnp.float32)
            days[c, :, :width] = shock
            days[c, :, width:] = (0.5 * (wide * wide)).astype(jnp.bfloat16)

    for i in range(chunk):
        slot = step * chunk + i

        @pl.when(slot < live[0])
        def _():
            tile = lax.rem(desks[slot] - position + (REACH + devices), devices)
            block = jnp.concatenate([delta_ref[i], gamma_ref[i]], axis=1)
            tiles_ref[tile] += lax.dot_general(
                days[columns[slot]], block, (((1,), (1,)), ((), ())),
                preferred_element_type=jnp.float32,
            )


def split(value):
    high = value.astype(jnp.bfloat16)
    return high, (value - high.astype(jnp.float32)).astype(jnp.bfloat16)


def exchange_kernel(n, scale, ids_ref, tiles, pnl_ref, book_ref, even, paired, landed, rows, pick,
                    load_sem, send1, recv1, send2, recv2, send3, recv3):
    me = lax.axis_index("factor")
    core = lax.rem(me, 2)
    sibling = me + 1 - 2 * core

    def at(distance):
        return {"factor": lax.rem(me + distance + n, n)}

    loads = [pltpu.make_async_copy(tiles.at[2 * e], even.at[e], load_sem.at[e]) for e in range(5)]
    for load in loads:
        load.start()

    barrier = pltpu.get_barrier_semaphore()
    for k in range(1, n):
        pl.semaphore_signal(barrier, inc=1, device_id=at(k), device_id_type=pl.DeviceIdType.MESH)
    pl.semaphore_wait(barrier, n - 1)

    pair = [
        pltpu.make_async_remote_copy(
            src_ref=tiles.at[2 * i + 1], dst_ref=paired.at[i],
            send_sem=send1.at[i], recv_sem=recv1.at[i],
            device_id={"factor": sibling}, device_id_type=pl.DeviceIdType.MESH,
        )
        for i in range(4)
    ]
    for i in (3, 0, 1, 2):
        pair[i].start()
    for load in loads:
        load.wait()

    def add_pair(e):
        i = e - 1 + core
        pltpu.make_async_remote_copy(
            src_ref=tiles.at[1], dst_ref=paired.at[i],
            send_sem=send1.at[i], recv_sem=recv1.at[i],
            device_id={"factor": sibling}, device_id_type=pl.DeviceIdType.MESH,
        ).wait_recv()
        even[e] += paired[i]

    out = []
    for s, e in enumerate((0, 4, 1, 3)):
        if e == 0:
            pl.when(core == 1)(functools.partial(add_pair, e))
        elif e == 4:
            pl.when(core == 0)(functools.partial(add_pair, e))
        else:
            add_pair(e)
        copy = pltpu.make_async_remote_copy(
            src_ref=even.at[e], dst_ref=landed.at[s],
            send_sem=send2.at[s], recv_sem=recv2.at[s],
            device_id=at(2 * e - 4), device_id_type=pl.DeviceIdType.MESH,
        )
        copy.start()
        out.append(copy)
    add_pair(2)

    whole = (even[0] + even[1]) + (even[2] + even[3]) + even[4]
    rows[0] = jnp.sum(whole.T, axis=0, keepdims=True)
    share = []
    for k in range(1, n):
        copy = pltpu.make_async_remote_copy(
            src_ref=rows.at[0], dst_ref=rows.at[k],
            send_sem=send3.at[k], recv_sem=recv3.at[k],
            device_id=at(k), device_id_type=pl.DeviceIdType.MESH,
        )
        copy.start()
        share.append(copy)
    day = lax.broadcasted_iota(jnp.int32, pick.shape, 0)
    pick[...] = (day == ids_ref[...]).astype(jnp.float32).astype(jnp.bfloat16)
    for copy in share:
        copy.wait()
    total = rows[0]
    for k in range(1, n):
        total += rows[k]
    high, rest = split(jnp.broadcast_to(total, (16, total.shape[1])))
    book = jnp.dot(high, pick[...], preferred_element_type=jnp.float32)
    book += jnp.dot(rest, pick[...], preferred_element_type=jnp.float32)
    book_ref[...] = book[0:1] * scale

    final = even[2]
    for s, copy in enumerate(out):
        copy.wait()
        final += landed[s]
    high, rest = split(final.T)
    pnl_ref[...] = jnp.dot(high, pick[...], preferred_element_type=jnp.float32) + jnp.dot(
        rest, pick[...], preferred_element_type=jnp.float32
    )
    for copy in pair:
        copy.wait_send()


def per_device(devices, history, scenario_ids, desk_ids, column_ids, live_count, delta_blocks, gamma_blocks):
    day_count, factors = history.shape
    slots, desk_rows, width = delta_blocks.shape
    columns = factors // width
    scenarios = scenario_ids.shape[0]

    tiles = pl.pallas_call(
        functools.partial(block_kernel, devices),
        grid_spec=pltpu.PrefetchScalarGridSpec(
            num_scalar_prefetch=3,
            grid=(slots // CHUNK,),
            in_specs=[
                pl.BlockSpec((day_count, factors), lambda g, *_: (0, 0)),
                pl.BlockSpec((CHUNK, desk_rows, width), lambda g, *_: (g, 0, 0)),
                pl.BlockSpec((CHUNK, desk_rows, width), lambda g, *_: (g, 0, 0)),
            ],
            out_specs=pl.BlockSpec((SPAN, day_count, desk_rows), lambda g, *_: (0, 0, 0)),
            scratch_shapes=[pltpu.VMEM((columns, day_count, 2 * width), jnp.bfloat16)],
        ),
        out_shape=jax.ShapeDtypeStruct((SPAN, day_count, desk_rows), jnp.float32),
        compiler_params=pltpu.CompilerParams(vmem_limit_bytes=40 * MIB),
        name="block_products",
    )(desk_ids, column_ids, live_count, history, delta_blocks, gamma_blocks)

    f32 = jnp.float32
    tile = (day_count, desk_rows)
    pnl, book = pl.pallas_call(
        functools.partial(exchange_kernel, devices, 1.0 / math.sqrt(devices * desk_rows)),
        in_specs=[pl.BlockSpec(memory_space=pltpu.VMEM), pl.BlockSpec(memory_space=pl.ANY)],
        out_specs=[pl.BlockSpec(memory_space=pltpu.VMEM)] * 2,
        out_shape=[
            jax.ShapeDtypeStruct((desk_rows, scenarios), f32),
            jax.ShapeDtypeStruct((1, scenarios), f32),
        ],
        scratch_shapes=[
            pltpu.VMEM((5, *tile), f32),
            pltpu.VMEM((4, *tile), f32),
            pltpu.VMEM((4, *tile), f32),
            pltpu.VMEM((devices, 1, day_count), f32),
            pltpu.VMEM((day_count, scenarios), jnp.bfloat16),
            pltpu.SemaphoreType.DMA((5,)),
            pltpu.SemaphoreType.DMA((4,)),
            pltpu.SemaphoreType.DMA((4,)),
            pltpu.SemaphoreType.DMA((4,)),
            pltpu.SemaphoreType.DMA((4,)),
            pltpu.SemaphoreType.DMA((devices,)),
            pltpu.SemaphoreType.DMA((devices,)),
        ],
        compiler_params=pltpu.CompilerParams(
            collective_id=0, has_side_effects=True, vmem_limit_bytes=40 * MIB
        ),
        name="desk_exchange",
    )(scenario_ids.reshape(1, scenarios), tiles)
    return pnl, book.reshape(scenarios)


def solution(mesh):
    return jax.shard_map(
        functools.partial(per_device, mesh.shape["factor"]),
        mesh=mesh,
        in_specs=(
            P(None, "factor"),
            P("groups"),
            P(("groups", "factor")),
            P(("groups", "factor")),
            P(("groups", "factor")),
            P(("groups", "factor"), None, None),
            P(("groups", "factor"), None, None),
        ),
        out_specs=(P(("groups", "factor"), None), P("groups")),
        check_vma=False,
    )
```

time: 1170 us -> 75.8 us (0.06)
  the two profiles are of different devices: /device:TPU:3 before, /device:TPU:0 now
where the time goes in v1:
time: 75.8 us; the launch traced here: 75.6 us
  Pallas kernels  65.5 us (86%)
  local copies, waits for them, and re-layouts  8.81 us (12%)
  between operations  1.32 us (2%)
    pallas_call x1, Pallas kernels, per_device(): pl.pallas_call(functools.partial(exchange_kernel, devices, 1.0 / math.sqr...  55.8 us
    pallas_call x1, Pallas kernels, per_device(): pl.pallas_call(functools.partial(block_kernel, devices), grid_spec=pltpu....  9.7 us
    unnamed x14, local copies, waits for them, and re-layouts  8.81 us

profile of v1, /device:TPU:0, one launch (start us, length us, event | category | flops | bytes accessed | tf_op | source)
XLA Modules:
  0.0 75.6 jit_solution(15555100253477482143)
XLA Ops:
  1.3 0.0 copy-start
  1.3 2.2 %copy-done = bf16[128,128,128]{2,1,0:T(8,128)(2,1)S(1)} copy-done((bf16[128,128,128]{2,1,0:T(8,128)(2,1)S(1)}, bf16[128,128,128]{2,1,0:T(8,128)(2,1)}, u32[]{:S(2)}) %copy-start) | copy-done | bytes 4194328
  3.5 0.0 copy-start.1
  3.5 2.2 %copy-done.1 = bf16[128,128,128]{2,1,0:T(8,128)(2,1)S(1)} copy-done((bf16[128,128,128]{2,1,0:T(8,128)(2,1)S(1)}, bf16[128,128,128]{2,1,0:T(8,128)(2,1)}, u32[]{:S(2)}) %copy-start.1) | copy-done | bytes 4194328
  5.7 0.0 copy-start.2
  5.7 1.7 %copy-done.2 = bf16[640,2048]{1,0:T(8,128)(2,1)S(1)} copy-done((bf16[640,2048]{1,0:T(8,128)(2,1)S(1)}, bf16[640,2048]{1,0:T(8,128)(2,1)}, u32[]{:S(2)}) %copy-start.2) | copy-done | bytes 2621464
  7.4 0.0 copy-start.4
  7.4 0.7 copy-done.4
  8.1 0.0 copy-start.5
  8.1 0.7 copy-done.5
  8.7 0.0 copy-start.3
  8.7 9.7 %block_products.1.tiles = f32[9,640,128]{2,1,0:T(8,128)S(1)} custom-call(s32[128]{0:T(128)S(1)} %copy-done.4, s32[128]{0:T(128)S(1)} %copy-done.5, s32[1]{0:T(128)S(6)} %copy.11.live, bf16[640,2048]{1,0:T(8,128)(2,1)S(1)} %copy-done.2, bf16[128,128,128]{2,1,0:T(8,128)(2,1)S(1)} %copy-done, bf16[128,128,128]{2,1,0:T(8,128)(2,1)S(1)} %copy-done.1), custom_call_target="tpu_custom_call" | custom-call | tf_op jit(solution)/shard_map/block_products/pallas_call | solution.py:147
  18.4 0.0 copy-done.3
  18.4 55.8 %desk_exchange.1 = (f32[128,1024]{1,0:T(8,128)S(1)}, f32[1,1024]{1,0:T(1,128)S(1)}) custom-call(s32[1,1024]{1,0:T(1,128)S(1)} %bitcast.2, f32[9,640,128]{2,1,0:T(8,128)S(1)} %block_products.1.tiles), custom_call_target="tpu_custom_call" | custom-call | tf_op jit(solution)/shard_map/desk_exchange/pallas_call | solution.py:167
  74.2 0.8 %copy.12 = f32[128,1024]{1,0:T(8,128)} copy(f32[128,1024]{1,0:T(8,128)S(1)} %get-tuple-element.8) | data formatting | bytes 1048576
  75.0 0.6 copy.13
Async XLA Ops:
  1.3 2.2 %copy-start = (bf16[128,128,128]{2,1,0:T(8,128)(2,1)S(1)}, bf16[128,128,128]{2,1,0:T(8,128)(2,1)}, u32[]{:S(2)}) copy-start(bf16[128,128,128]{2,1,0:T(8,128)(2,1)} %delta_ref.1) | copy-start | bytes 12582916
  3.5 2.2 %copy-start.1 = (bf16[128,128,128]{2,1,0:T(8,128)(2,1)S(1)}, bf16[128,128,128]{2,1,0:T(8,128)(2,1)}, u32[]{:S(2)}) copy-start(bf16[128,128,128]{2,1,0:T(8,128)(2,1)} %gamma_ref.1) | copy-start | bytes 12582916
  5.7 1.7 %copy-start.2 = (bf16[640,2048]{1,0:T(8,128)(2,1)S(1)}, bf16[640,2048]{1,0:T(8,128)(2,1)}, u32[]{:S(2)}) copy-start(bf16[640,2048]{1,0:T(8,128)(2,1)} %hist_ref.1) | copy-start | bytes 7864324
  7.4 0.7 copy-start.4
  8.1 0.7 copy-start.5
  8.7 9.7 %copy-start.3 = (s32[1024]{0:T(1024)S(1)}, s32[1024]{0:T(1024)}, u32[]{:S(2)}) copy-start(s32[1024]{0:T(1024)} %param.8) | copy-start | bytes 12292

commit v2 on v1

--- a/solution.py
+++ b/solution.py
@@ -10,7 +10,8 @@
 
 REACH = 4
 SPAN = 2 * REACH + 1
-CHUNK = 8
+CHUNK = 16
+BATCH = 8
 MIB = 1 << 20
 
 
@@ -28,17 +29,19 @@
             days[c, :, :width] = shock
             days[c, :, width:] = (0.5 * (wide * wide)).astype(jnp.bfloat16)
 
-    for i in range(chunk):
-        slot = step * chunk + i
-
-        @pl.when(slot < live[0])
+    for base in range(0, chunk, BATCH):
+
+        @pl.when(step * chunk + base < live[0])
         def _():
-            tile = lax.rem(desks[slot] - position + (REACH + devices), devices)
-            block = jnp.concatenate([delta_ref[i], gamma_ref[i]], axis=1)
-            tiles_ref[tile] += lax.dot_general(
-                days[columns[slot]], block, (((1,), (1,)), ((), ())),
-                preferred_element_type=jnp.float32,
-            )
+            for i in range(base, base + BATCH):
+                slot = step * chunk + i
+                tile = lax.rem(desks[slot] - position + (REACH + devices), devices)
+                block = jnp.concatenate([delta_ref[i], gamma_ref[i]], axis=1)
+                block = jnp.where(slot < live[0], block, jnp.zeros_like(block))
+                tiles_ref[tile] += lax.dot_general(
+                    days[columns[slot]], block, (((1,), (1,)), ((), ())),
+                    preferred_element_type=jnp.float32,
+                )
 
 
 def split(value):
@@ -46,14 +49,27 @@
     return high, (value - high.astype(jnp.float32)).astype(jnp.bfloat16)
 
 
-def exchange_kernel(n, scale, ids_ref, tiles, pnl_ref, book_ref, even, paired, landed, rows, pick,
-                    load_sem, send1, recv1, send2, recv2, send3, recv3):
+def exchange_kernel(n, scale, ids_ref, tiles, pnl_ref, book_ref, even, paired, middle, landed, rows, pick,
+                    load_sem, send1, recv1, send2, recv2, send3, recv3, send4, recv4):
     me = lax.axis_index("factor")
     core = lax.rem(me, 2)
+    side = lax.rem(me // 2, 2)
     sibling = me + 1 - 2 * core
+    partner = me + 2 - 4 * side
+    half = even.shape[1] // 2
+    parts = [pl.ds(h * half, half) for h in range(2)]
 
     def at(distance):
         return {"factor": lax.rem(me + distance + n, n)}
+
+    def remote(src, dst, send, recv, device):
+        return pltpu.make_async_remote_copy(
+            src_ref=src, dst_ref=dst, send_sem=send, recv_sem=recv,
+            device_id=device, device_id_type=pl.DeviceIdType.MESH,
+        )
+
+    def place(k):
+        return k + side * (4 - 2 * k)
 
     loads = [pltpu.make_async_copy(tiles.at[2 * e], even.at[e], load_sem.at[e]) for e in range(5)]
     for load in loads:
@@ -64,56 +80,69 @@
         pl.semaphore_signal(barrier, inc=1, device_id=at(k), device_id_type=pl.DeviceIdType.MESH)
     pl.semaphore_wait(barrier, n - 1)
 
-    pair = [
-        pltpu.make_async_remote_copy(
-            src_ref=tiles.at[2 * i + 1], dst_ref=paired.at[i],
-            send_sem=send1.at[i], recv_sem=recv1.at[i],
-            device_id={"factor": sibling}, device_id_type=pl.DeviceIdType.MESH,
-        )
-        for i in range(4)
-    ]
-    for i in (3, 0, 1, 2):
-        pair[i].start()
+    def pair(i):
+        return remote(tiles.at[2 * i + 1], paired.at[i], send1.at[i], recv1.at[i], {"factor": sibling})
+
+    def if_paired(k, owner, act):
+        if k == 0:
+            pl.when(owner == 1 - side)(act)
+        elif k == 4:
+            pl.when(owner == side)(act)
+        else:
+            act()
+
+    order = (0, 1, 3, 4, 2)
+    for k in order:
+        if_paired(k, 1 - core, lambda: pair(place(k) - core).start())
     for load in loads:
         load.wait()
 
-    def add_pair(e):
-        i = e - 1 + core
-        pltpu.make_async_remote_copy(
-            src_ref=tiles.at[1], dst_ref=paired.at[i],
-            send_sem=send1.at[i], recv_sem=recv1.at[i],
-            device_id={"factor": sibling}, device_id_type=pl.DeviceIdType.MESH,
-        ).wait_recv()
-        even[e] += paired[i]
-
-    out = []
-    for s, e in enumerate((0, 4, 1, 3)):
-        if e == 0:
-            pl.when(core == 1)(functools.partial(add_pair, e))
-        elif e == 4:
-            pl.when(core == 0)(functools.partial(add_pair, e))
-        else:
-            add_pair(e)
-        copy = pltpu.make_async_remote_copy(
-            src_ref=even.at[e], dst_ref=landed.at[s],
-            send_sem=send2.at[s], recv_sem=recv2.at[s],
-            device_id=at(2 * e - 4), device_id_type=pl.DeviceIdType.MESH,
-        )
-        copy.start()
-        out.append(copy)
+    def add_pair(k):
+        e = place(k)
+
+        def act():
+            i = e - 1 + core
+            pair(i).wait_recv()
+            even[e] += paired[i]
+
+        if_paired(k, core, act)
+
+    def straight(k, slot, part):
+        e = place(k)
+        return remote(even.at[e, part], landed.at[slot, part], send2.at[slot, part.start // half],
+                      recv2.at[slot, part.start // half], at(2 * e - 4))
+
+    def across(k, slot, part):
+        return remote(even.at[place(k), part], middle.at[slot, part], send3.at[slot, part.start // half],
+                      recv3.at[slot, part.start // half], {"factor": partner})
+
+    add_pair(0)
+    first = [straight(0, 0, part) for part in parts]
+    for copy in first:
+        copy.start()
+    add_pair(1)
+    joined = [across(1, 0, part) for part in parts]
+    for copy in joined:
+        copy.start()
+    add_pair(3)
+    owned = [across(3, 1, part) for part in parts]
+    for copy in owned:
+        copy.start()
+    add_pair(4)
     add_pair(2)
 
     whole = (even[0] + even[1]) + (even[2] + even[3]) + even[4]
     rows[0] = jnp.sum(whole.T, axis=0, keepdims=True)
-    share = []
-    for k in range(1, n):
-        copy = pltpu.make_async_remote_copy(
-            src_ref=rows.at[0], dst_ref=rows.at[k],
-            send_sem=send3.at[k], recv_sem=recv3.at[k],
-            device_id=at(k), device_id_type=pl.DeviceIdType.MESH,
-        )
-        copy.start()
-        share.append(copy)
+    share = [remote(rows.at[0], rows.at[k], send4.at[k], recv4.at[k], at(k)) for k in range(1, n)]
+
+    second = [straight(4, 1, part) for part in parts]
+    for h, part in enumerate(parts):
+        joined[h].wait_recv()
+        even[place(4), part] += middle[0, part]
+        second[h].start()
+    for copy in share:
+        copy.start()
+
     day = lax.broadcasted_iota(jnp.int32, pick.shape, 0)
     pick[...] = (day == ids_ref[...]).astype(jnp.float32).astype(jnp.bfloat16)
     for copy in share:
@@ -126,16 +155,19 @@
     book += jnp.dot(rest, pick[...], preferred_element_type=jnp.float32)
     book_ref[...] = book[0:1] * scale
 
-    final = even[2]
-    for s, copy in enumerate(out):
+    for copy in owned + first:
         copy.wait()
-        final += landed[s]
-    high, rest = split(final.T)
+    even[2] += middle[1] + landed[0]
+    for copy in second:
+        copy.wait()
+    high, rest = split((even[2] + landed[1]).T)
     pnl_ref[...] = jnp.dot(high, pick[...], preferred_element_type=jnp.float32) + jnp.dot(
         rest, pick[...], preferred_element_type=jnp.float32
     )
-    for copy in pair:
+    for copy in joined:
         copy.wait_send()
+    for k in order:
+        if_paired(k, 1 - core, lambda: pair(place(k) - core).wait_send())
 
 
 def per_device(devices, history, scenario_ids, desk_ids, column_ids, live_count, delta_blocks, gamma_blocks):
@@ -158,7 +190,7 @@
             scratch_shapes=[pltpu.VMEM((columns, day_count, 2 * width), jnp.bfloat16)],
         ),
         out_shape=jax.ShapeDtypeStruct((SPAN, day_count, desk_rows), jnp.float32),
-        compiler_params=pltpu.CompilerParams(vmem_limit_bytes=40 * MIB),
+        compiler_params=pltpu.CompilerParams(vmem_limit_bytes=60 * MIB),
         name="block_products",
     )(desk_ids, column_ids, live_count, history, delta_blocks, gamma_blocks)
 
@@ -175,14 +207,17 @@
         scratch_shapes=[
             pltpu.VMEM((5, *tile), f32),
             pltpu.VMEM((4, *tile), f32),
-            pltpu.VMEM((4, *tile), f32),
+            pltpu.VMEM((2, *tile), f32),
+            pltpu.VMEM((2, *tile), f32),
             pltpu.VMEM((devices, 1, day_count), f32),
             pltpu.VMEM((day_count, scenarios), jnp.bfloat16),
             pltpu.SemaphoreType.DMA((5,)),
             pltpu.SemaphoreType.DMA((4,)),
             pltpu.SemaphoreType.DMA((4,)),
-            pltpu.SemaphoreType.DMA((4,)),
-            pltpu.SemaphoreType.DMA((4,)),
+            pltpu.SemaphoreType.DMA((2, 2)),
+            pltpu.SemaphoreType.DMA((2, 2)),
+            pltpu.SemaphoreType.DMA((2, 2)),
+            pltpu.SemaphoreType.DMA((2, 2)),
             pltpu.SemaphoreType.DMA((devices,)),
             pltpu.SemaphoreType.DMA((devices,)),
         ],

time: 75.8 us -> 51.1 us (0.67)
  Pallas kernels: 65.5 us -> 45.8 us
  local copies, waits for them, and re-layouts: 8.81 us -> 3.23 us
    pallas_call x1, Pallas kernels: 55.8 us -> 34.1 us  [per_device(): pl.pallas_call(functools.partial(exchange_kernel, devices, 1.0 / math.sqr...]
    unnamed x14 -> x6, local copies, waits for them, and re-layouts: 8.81 us -> 3.23 us
    pallas_call x1, Pallas kernels: 9.7 us -> 11.7 us  [per_device(): pl.pallas_call(functools.partial(block_kernel, devices), grid_spec=pltpu....]
where the time goes in v2:
time: 51.1 us; the launch traced here: 50.4 us
  Pallas kernels  45.8 us (90%)
  local copies, waits for them, and re-layouts  3.23 us (6%)
  between operations  1.3 us (3%)
    pallas_call x1, Pallas kernels, per_device(): pl.pallas_call(functools.partial(exchange_kernel, devices, 1.0 / math.sqr...  34.1 us
    pallas_call x1, Pallas kernels, per_device(): pl.pallas_call(functools.partial(block_kernel, devices), grid_spec=pltpu....  11.7 us
    unnamed x6, local copies, waits for them, and re-layouts  3.23 us

profile of v2, /device:TPU:0, one launch (start us, length us, event | category | flops | bytes accessed | tf_op | source)
XLA Modules:
  0.0 50.4 jit_solution(3282540155957432755)
XLA Ops:
  1.3 0.0 copy-start.1
  1.3 11.7 %block_products.1.tiles = f32[9,640,128]{2,1,0:T(8,128)} custom-call(s32[128]{0:T(128)} %desks.1, s32[128]{0:T(128)} %columns.1, s32[1]{0:T(128)S(6)} %copy.11.live, bf16[640,2048]{1,0:T(8,128)(2,1)} %hist_ref.1, bf16[128,128,128]{2,1,0:T(8,128)(2,1)} %delta_ref.1, bf16[128,128,128]{2,1,0:T(8,128)(2,1)} %gamma_ref.1), custom_call_target="tpu_custom_call" | custom-call | tf_op jit(solution)/shard_map/block_products/pallas_call | solution.py:179
  13.0 0.0 copy-done.1
  13.0 0.0 copy-start
  13.0 1.8 %copy-done = f32[9,640,128]{2,1,0:T(8,128)S(1)} copy-done((f32[9,640,128]{2,1,0:T(8,128)S(1)}, f32[9,640,128]{2,1,0:T(8,128)}, u32[]{:S(2)}) %copy-start) | copy-done | bytes 2949144
  14.9 34.1 %desk_exchange.1 = (f32[128,1024]{1,0:T(8,128)S(1)}, f32[1,1024]{1,0:T(1,128)S(1)}) custom-call(s32[1,1024]{1,0:T(1,128)S(1)} %bitcast.2, f32[9,640,128]{2,1,0:T(8,128)S(1)} %copy-done), custom_call_target="tpu_custom_call" | custom-call | tf_op jit(solution)/shard_map/desk_exchange/pallas_call | solution.py:199
  49.0 0.8 %copy.12 = f32[128,1024]{1,0:T(8,128)} copy(f32[128,1024]{1,0:T(8,128)S(1)} %get-tuple-element.8) | data formatting | bytes 1048576
  49.8 0.6 %copy.13 = f32[1024]{0:T(1024)} copy(f32[1024]{0:T(1024)S(1)} %bitcast.3) | data formatting | bytes 8192
Async XLA Ops:
  1.3 11.8 %copy-start.1 = (s32[1024]{0:T(1024)S(1)}, s32[1024]{0:T(1024)}, u32[]{:S(2)}) copy-start(s32[1024]{0:T(1024)} %param.8) | copy-start | bytes 12292
  13.0 1.8 %copy-start = (f32[9,640,128]{2,1,0:T(8,128)S(1)}, f32[9,640,128]{2,1,0:T(8,128)}, u32[]{:S(2)}) copy-start(f32[9,640,128]{2,1,0:T(8,128)} %block_products.1.tiles) | copy-start | bytes 8847364

commit v3 on v2

--- a/solution.py
+++ b/solution.py
@@ -11,37 +11,66 @@
 REACH = 4
 SPAN = 2 * REACH + 1
 CHUNK = 16
-BATCH = 8
+HIST_PARTS = 4
+PIECES = 4
 MIB = 1 << 20
 
 
-def block_kernel(devices, desks, columns, live, hist_ref, delta_ref, gamma_ref, tiles_ref, days):
-    step = pl.program_id(0)
+def block_kernel(devices, desks, columns, live, hist_hbm, delta_hbm, gamma_hbm, out_hbm,
+                 tiles, days, hist, delta, gamma, hist_sem, block_sem, out_sem):
     position = lax.axis_index("factor")
-    chunk, _, width = delta_ref.shape
-
-    @pl.when(step == 0)
-    def _():
-        tiles_ref[...] = jnp.zeros_like(tiles_ref)
-        for c in range(days.shape[0]):
-            shock = hist_ref[:, c * width:(c + 1) * width]
+    slots, _, width = delta.shape
+    span = hist.shape[1] // hist_sem.shape[0]
+
+    def hist_copy(h):
+        at = pl.ds(h * span, span)
+        return pltpu.make_async_copy(hist_hbm.at[:, at], hist.at[:, at], hist_sem.at[h])
+
+    def block_copies(g):
+        at = pl.ds(g * CHUNK, CHUNK)
+        return [
+            pltpu.make_async_copy(delta_hbm.at[at], delta.at[at], block_sem.at[0, g]),
+            pltpu.make_async_copy(gamma_hbm.at[at], gamma.at[at], block_sem.at[1, g]),
+        ]
+
+    for h in range(hist_sem.shape[0]):
+        hist_copy(h).start()
+    for g in range(slots // CHUNK):
+
+        @pl.when(g * CHUNK < live[0])
+        def _():
+            for copy in block_copies(g):
+                copy.start()
+
+    tiles[...] = jnp.zeros_like(tiles)
+    for h in range(hist_sem.shape[0]):
+        hist_copy(h).wait()
+        for c in range(h * span // width, (h + 1) * span // width):
+            shock = hist[:, c * width:(c + 1) * width]
             wide = shock.astype(jnp.float32)
-            days[c, :, :width] = shock
-            days[c, :, width:] = (0.5 * (wide * wide)).astype(jnp.bfloat16)
-
-    for base in range(0, chunk, BATCH):
-
-        @pl.when(step * chunk + base < live[0])
+            days[c, :width, :] = shock.T
+            days[c, width:, :] = (0.5 * (wide * wide)).astype(jnp.bfloat16).T
+
+    def chunk_step(g, carry):
+        @pl.when(g * CHUNK < live[0])
         def _():
-            for i in range(base, base + BATCH):
-                slot = step * chunk + i
+            for copy in block_copies(g):
+                copy.wait()
+            for i in range(CHUNK):
+                slot = g * CHUNK + i
                 tile = lax.rem(desks[slot] - position + (REACH + devices), devices)
-                block = jnp.concatenate([delta_ref[i], gamma_ref[i]], axis=1)
+                block = jnp.concatenate([delta[slot], gamma[slot]], axis=1)
                 block = jnp.where(slot < live[0], block, jnp.zeros_like(block))
-                tiles_ref[tile] += lax.dot_general(
-                    days[columns[slot]], block, (((1,), (1,)), ((), ())),
-                    preferred_element_type=jnp.float32,
-                )
+                tiles[tile] += jnp.dot(block, days[columns[slot]], preferred_element_type=jnp.float32)
+
+        return carry
+
+    lax.fori_loop(0, slots // CHUNK, chunk_step, 0)
+    copies = [pltpu.make_async_copy(tiles.at[t], out_hbm.at[t], out_sem.at[t]) for t in range(SPAN)]
+    for copy in copies:
+        copy.start()
+    for copy in copies:
+        copy.wait()
 
 
 def split(value):
@@ -56,8 +85,8 @@
     side = lax.rem(me // 2, 2)
     sibling = me + 1 - 2 * core
     partner = me + 2 - 4 * side
-    half = even.shape[1] // 2
-    parts = [pl.ds(h * half, half) for h in range(2)]
+    half = even.shape[1] // PIECES
+    parts = [pl.ds(h * half, half) for h in range(PIECES)]
 
     def at(distance):
         return {"factor": lax.rem(me + distance + n, n)}
@@ -76,9 +105,9 @@
         load.start()
 
     barrier = pltpu.get_barrier_semaphore()
-    for k in range(1, n):
-        pl.semaphore_signal(barrier, inc=1, device_id=at(k), device_id_type=pl.DeviceIdType.MESH)
-    pl.semaphore_wait(barrier, n - 1)
+    for device in ({"factor": sibling}, {"factor": partner}, at(4), at(-4)):
+        pl.semaphore_signal(barrier, inc=1, device_id=device, device_id_type=pl.DeviceIdType.MESH)
+    pl.semaphore_wait(barrier, 4)
 
     def pair(i):
         return remote(tiles.at[2 * i + 1], paired.at[i], send1.at[i], recv1.at[i], {"factor": sibling})
@@ -132,24 +161,31 @@
     add_pair(2)
 
     whole = (even[0] + even[1]) + (even[2] + even[3]) + even[4]
-    rows[0] = jnp.sum(whole.T, axis=0, keepdims=True)
-    share = [remote(rows.at[0], rows.at[k], send4.at[k], recv4.at[k], at(k)) for k in range(1, n)]
+    rows[0] = jnp.sum(whole, axis=0, keepdims=True)
+    near = [
+        remote(rows.at[0], rows.at[1], send4.at[0], recv4.at[0], {"factor": sibling}),
+        remote(rows.at[2], rows.at[3], send4.at[1], recv4.at[1], {"factor": partner}),
+    ]
+    near[0].start()
 
     second = [straight(4, 1, part) for part in parts]
     for h, part in enumerate(parts):
         joined[h].wait_recv()
         even[place(4), part] += middle[0, part]
         second[h].start()
-    for copy in share:
-        copy.start()
-
     day = lax.broadcasted_iota(jnp.int32, pick.shape, 0)
     pick[...] = (day == ids_ref[...]).astype(jnp.float32).astype(jnp.bfloat16)
-    for copy in share:
-        copy.wait()
-    total = rows[0]
-    for k in range(1, n):
-        total += rows[k]
+    near[0].wait()
+    rows[2] = rows[0] + rows[1]
+    near[1].start()
+    near[1].wait()
+    rows[4] = rows[2] + rows[3]
+    total = rows[4]
+    for k in range(n // 4 - 1):
+        hop = remote(rows.at[4 + k], rows.at[5 + k], send4.at[2 + k], recv4.at[2 + k], at(4))
+        hop.start()
+        hop.wait()
+        total += rows[5 + k]
     high, rest = split(jnp.broadcast_to(total, (16, total.shape[1])))
     book = jnp.dot(high, pick[...], preferred_element_type=jnp.float32)
     book += jnp.dot(rest, pick[...], preferred_element_type=jnp.float32)
@@ -160,7 +196,7 @@
     even[2] += middle[1] + landed[0]
     for copy in second:
         copy.wait()
-    high, rest = split((even[2] + landed[1]).T)
+    high, rest = split(even[2] + landed[1])
     pnl_ref[...] = jnp.dot(high, pick[...], preferred_element_type=jnp.float32) + jnp.dot(
         rest, pick[...], preferred_element_type=jnp.float32
     )
@@ -178,24 +214,25 @@
 
     tiles = pl.pallas_call(
         functools.partial(block_kernel, devices),
-        grid_spec=pltpu.PrefetchScalarGridSpec(
-            num_scalar_prefetch=3,
-            grid=(slots // CHUNK,),
-            in_specs=[
-                pl.BlockSpec((day_count, factors), lambda g, *_: (0, 0)),
-                pl.BlockSpec((CHUNK, desk_rows, width), lambda g, *_: (g, 0, 0)),
-                pl.BlockSpec((CHUNK, desk_rows, width), lambda g, *_: (g, 0, 0)),
-            ],
-            out_specs=pl.BlockSpec((SPAN, day_count, desk_rows), lambda g, *_: (0, 0, 0)),
-            scratch_shapes=[pltpu.VMEM((columns, day_count, 2 * width), jnp.bfloat16)],
-        ),
-        out_shape=jax.ShapeDtypeStruct((SPAN, day_count, desk_rows), jnp.float32),
-        compiler_params=pltpu.CompilerParams(vmem_limit_bytes=60 * MIB),
+        in_specs=[pl.BlockSpec(memory_space=pltpu.SMEM)] * 3 + [pl.BlockSpec(memory_space=pl.ANY)] * 3,
+        out_specs=pl.BlockSpec(memory_space=pl.ANY),
+        scratch_shapes=[
+            pltpu.VMEM((SPAN, desk_rows, day_count), jnp.float32),
+            pltpu.VMEM((columns, 2 * width, day_count), jnp.bfloat16),
+            pltpu.VMEM((day_count, factors), jnp.bfloat16),
+            pltpu.VMEM((slots, desk_rows, width), jnp.bfloat16),
+            pltpu.VMEM((slots, desk_rows, width), jnp.bfloat16),
+            pltpu.SemaphoreType.DMA((HIST_PARTS,)),
+            pltpu.SemaphoreType.DMA((2, slots // CHUNK)),
+            pltpu.SemaphoreType.DMA((SPAN,)),
+        ],
+        out_shape=jax.ShapeDtypeStruct((SPAN, desk_rows, day_count), jnp.float32),
+        compiler_params=pltpu.CompilerParams(vmem_limit_bytes=62 * MIB),
         name="block_products",
     )(desk_ids, column_ids, live_count, history, delta_blocks, gamma_blocks)
 
     f32 = jnp.float32
-    tile = (day_count, desk_rows)
+    tile = (desk_rows, day_count)
     pnl, book = pl.pallas_call(
         functools.partial(exchange_kernel, devices, 1.0 / math.sqrt(devices * desk_rows)),
         in_specs=[pl.BlockSpec(memory_space=pltpu.VMEM), pl.BlockSpec(memory_space=pl.ANY)],
@@ -209,17 +246,17 @@
             pltpu.VMEM((4, *tile), f32),
             pltpu.VMEM((2, *tile), f32),
             pltpu.VMEM((2, *tile), f32),
-            pltpu.VMEM((devices, 1, day_count), f32),
+            pltpu.VMEM((devices // 4 + 4, 1, day_count), f32),
             pltpu.VMEM((day_count, scenarios), jnp.bfloat16),
             pltpu.SemaphoreType.DMA((5,)),
             pltpu.SemaphoreType.DMA((4,)),
             pltpu.SemaphoreType.DMA((4,)),
-            pltpu.SemaphoreType.DMA((2, 2)),
-            pltpu.SemaphoreType.DMA((2, 2)),
-            pltpu.SemaphoreType.DMA((2, 2)),
-            pltpu.SemaphoreType.DMA((2, 2)),
-            pltpu.SemaphoreType.DMA((devices,)),
-            pltpu.SemaphoreType.DMA((devices,)),
+            pltpu.SemaphoreType.DMA((2, PIECES)),
+            pltpu.SemaphoreType.DMA((2, PIECES)),
+            pltpu.SemaphoreType.DMA((2, PIECES)),
+            pltpu.SemaphoreType.DMA((2, PIECES)),
+            pltpu.SemaphoreType.DMA((devices // 4 + 1,)),
+            pltpu.SemaphoreType.DMA((devices // 4 + 1,)),
         ],
         compiler_params=pltpu.CompilerParams(
             collective_id=0, has_side_effects=True, vmem_limit_bytes=40 * MIB

time: 51.1 us -> 50.4 us (0.986); the launches traced: 50.4 us -> 50.4 us
    pallas_call x1, Pallas kernels: 34.1 us -> 35.1 us  [per_device(): pl.pallas_call(functools.partial(exchange_kernel, devices, 1.0 / math.sqr...]
    pallas_call x1, Pallas kernels: 11.7 us -> 10.8 us  [per_device(): pl.pallas_call(functools.partial(block_kernel, devices), in_specs=[pl.Blo...]
where the time goes in v3:
time: 50.4 us
  Pallas kernels  45.9 us (91%)
  local copies, waits for them, and re-layouts  3.22 us (6%)
  between operations  1.32 us (3%)
    pallas_call x1, Pallas kernels, per_device(): pl.pallas_call(functools.partial(exchange_kernel, devices, 1.0 / math.sqr...  35.1 us
    pallas_call x1, Pallas kernels, per_device(): pl.pallas_call(functools.partial(block_kernel, devices), in_specs=[pl.Blo...  10.8 us
    unnamed x6, local copies, waits for them, and re-layouts  3.22 us

profile of v3, /device:TPU:0, one launch (start us, length us, event | category | flops | bytes accessed | tf_op | source)
XLA Modules:
  0.0 50.4 jit_solution(18211532227163005906)
XLA Ops:
  1.3 0.0 copy-start.1
  1.3 10.8 %block_products.1.tiles = f32[9,128,640]{2,1,0:T(8,128)} custom-call(s32[128]{0:T(128)} %desks.1, s32[128]{0:T(128)} %columns.1, s32[1]{0:T(128)S(6)} %copy.11.live, bf16[640,2048]{1,0:T(8,128)(2,1)} %hist_hbm.1, bf16[128,128,128]{2,1,0:T(8,128)(2,1)} %delta_hbm.1, bf16[128,128,128]{2,1,0:T(8,128)(2,1)} %gamma_hbm.1), custom_call_target="tpu_custom_call" | custom-call | tf_op jit(solution)/shard_map/block_products/pallas_call | solution.py:215
  12.1 0.0 copy-done.1
  12.1 0.0 copy-start
  12.1 1.8 %copy-done = f32[9,128,640]{2,1,0:T(8,128)S(1)} copy-done((f32[9,128,640]{2,1,0:T(8,128)S(1)}, f32[9,128,640]{2,1,0:T(8,128)}, u32[]{:S(2)}) %copy-start) | copy-done | bytes 2949144
  13.9 35.1 %desk_exchange.1 = (f32[128,1024]{1,0:T(8,128)S(1)}, f32[1,1024]{1,0:T(1,128)S(1)}) custom-call(s32[1,1024]{1,0:T(1,128)S(1)} %bitcast.2, f32[9,128,640]{2,1,0:T(8,128)S(1)} %copy-done), custom_call_target="tpu_custom_call" | custom-call | tf_op jit(solution)/shard_map/desk_exchange/pallas_call | solution.py:236
  49.0 0.8 %copy.12 = f32[128,1024]{1,0:T(8,128)} copy(f32[128,1024]{1,0:T(8,128)S(1)} %get-tuple-element.8) | data formatting | bytes 1048576
  49.8 0.6 %copy.13 = f32[1024]{0:T(1024)} copy(f32[1024]{0:T(1024)S(1)} %bitcast.3) | data formatting | bytes 8192
Async XLA Ops:
  1.3 10.8 %copy-start.1 = (s32[1024]{0:T(1024)S(1)}, s32[1024]{0:T(1024)}, u32[]{:S(2)}) copy-start(s32[1024]{0:T(1024)} %param.8) | copy-start | bytes 12292
  12.1 1.8 %copy-start = (f32[9,128,640]{2,1,0:T(8,128)S(1)}, f32[9,128,640]{2,1,0:T(8,128)}, u32[]{:S(2)}) copy-start(f32[9,128,640]{2,1,0:T(8,128)} %block_products.1.tiles) | copy-start | bytes 8847364

commit v4 on v3

--- a/solution.py
+++ b/solution.py
@@ -12,7 +12,7 @@
 SPAN = 2 * REACH + 1
 CHUNK = 16
 HIST_PARTS = 4
-PIECES = 4
+PIECES = 2
 MIB = 1 << 20
 
 
@@ -105,9 +105,9 @@
         load.start()
 
     barrier = pltpu.get_barrier_semaphore()
-    for device in ({"factor": sibling}, {"factor": partner}, at(4), at(-4)):
-        pl.semaphore_signal(barrier, inc=1, device_id=device, device_id_type=pl.DeviceIdType.MESH)
-    pl.semaphore_wait(barrier, 4)
+    for k in range(1, n):
+        pl.semaphore_signal(barrier, inc=1, device_id=at(k), device_id_type=pl.DeviceIdType.MESH)
+    pl.semaphore_wait(barrier, n - 1)
 
     def pair(i):
         return remote(tiles.at[2 * i + 1], paired.at[i], send1.at[i], recv1.at[i], {"factor": sibling})
@@ -162,11 +162,9 @@
 
     whole = (even[0] + even[1]) + (even[2] + even[3]) + even[4]
     rows[0] = jnp.sum(whole, axis=0, keepdims=True)
-    near = [
-        remote(rows.at[0], rows.at[1], send4.at[0], recv4.at[0], {"factor": sibling}),
-        remote(rows.at[2], rows.at[3], send4.at[1], recv4.at[1], {"factor": partner}),
-    ]
-    near[0].start()
+    share = [remote(rows.at[0], rows.at[k], send4.at[k], recv4.at[k], at(k)) for k in range(1, n)]
+    for copy in share:
+        copy.start()
 
     second = [straight(4, 1, part) for part in parts]
     for h, part in enumerate(parts):
@@ -175,17 +173,11 @@
         second[h].start()
     day = lax.broadcasted_iota(jnp.int32, pick.shape, 0)
     pick[...] = (day == ids_ref[...]).astype(jnp.float32).astype(jnp.bfloat16)
-    near[0].wait()
-    rows[2] = rows[0] + rows[1]
-    near[1].start()
-    near[1].wait()
-    rows[4] = rows[2] + rows[3]
-    total = rows[4]
-    for k in range(n // 4 - 1):
-        hop = remote(rows.at[4 + k], rows.at[5 + k], send4.at[2 + k], recv4.at[2 + k], at(4))
-        hop.start()
-        hop.wait()
-        total += rows[5 + k]
+    for copy in share:
+        copy.wait()
+    total = rows[0]
+    for k in range(1, n):
+        total += rows[k]
     high, rest = split(jnp.broadcast_to(total, (16, total.shape[1])))
     book = jnp.dot(high, pick[...], preferred_element_type=jnp.float32)
     book += jnp.dot(rest, pick[...], preferred_element_type=jnp.float32)
@@ -227,7 +219,7 @@
             pltpu.SemaphoreType.DMA((SPAN,)),
         ],
         out_shape=jax.ShapeDtypeStruct((SPAN, desk_rows, day_count), jnp.float32),
-        compiler_params=pltpu.CompilerParams(vmem_limit_bytes=62 * MIB),
+        compiler_params=pltpu.CompilerParams(vmem_limit_bytes=63 * MIB),
         name="block_products",
     )(desk_ids, column_ids, live_count, history, delta_blocks, gamma_blocks)
 
@@ -246,7 +238,7 @@
             pltpu.VMEM((4, *tile), f32),
             pltpu.VMEM((2, *tile), f32),
             pltpu.VMEM((2, *tile), f32),
-            pltpu.VMEM((devices // 4 + 4, 1, day_count), f32),
+            pltpu.VMEM((devices, 1, day_count), f32),
             pltpu.VMEM((day_count, scenarios), jnp.bfloat16),
             pltpu.SemaphoreType.DMA((5,)),
             pltpu.SemaphoreType.DMA((4,)),
@@ -255,11 +247,11 @@
             pltpu.SemaphoreType.DMA((2, PIECES)),
             pltpu.SemaphoreType.DMA((2, PIECES)),
             pltpu.SemaphoreType.DMA((2, PIECES)),
-            pltpu.SemaphoreType.DMA((devices // 4 + 1,)),
-            pltpu.SemaphoreType.DMA((devices // 4 + 1,)),
+            pltpu.SemaphoreType.DMA((devices,)),
+            pltpu.SemaphoreType.DMA((devices,)),
         ],
         compiler_params=pltpu.CompilerParams(
-            collective_id=0, has_side_effects=True, vmem_limit_bytes=40 * MIB
+            collective_id=0, has_side_effects=True, vmem_limit_bytes=62 * MIB
         ),
         name="desk_exchange",
     )(scenario_ids.reshape(1, scenarios), tiles)

time: 50.4 us -> 45.2 us (0.90)
  Pallas kernels: 45.9 us -> 40.7 us
    pallas_call x1, Pallas kernels: 10.8 us -> 6.63 us  [per_device(): pl.pallas_call(functools.partial(block_kernel, devices), in_specs=[pl.Blo...]
    pallas_call x1, Pallas kernels: 35.1 us -> 34.1 us  [per_device(): pl.pallas_call(functools.partial(exchange_kernel, devices, 1.0 / math.sqr...]
    unnamed x6 -> x2, local copies, waits for them, and re-layouts: 3.22 us -> 3.16 us
where the time goes in v4:
time: 45.2 us
  Pallas kernels  40.7 us (90%)
  local copies, waits for them, and re-layouts  3.16 us (7%)
  between operations  1.29 us (3%)
    pallas_call x1, Pallas kernels, per_device(): pl.pallas_call(functools.partial(exchange_kernel, devices, 1.0 / math.sqr...  34.1 us
    pallas_call x1, Pallas kernels, per_device(): pl.pallas_call(functools.partial(block_kernel, devices), in_specs=[pl.Blo...  6.63 us
    unnamed x2, local copies, waits for them, and re-layouts  3.16 us

profile of v4, /device:TPU:0, one launch (start us, length us, event | category | flops | bytes accessed | tf_op | source)
XLA Modules:
  0.0 45.2 jit_solution(5498023505128031298)
XLA Ops:
  1.3 6.6 %block_products.1.tiles = f32[9,128,640]{2,1,0:T(8,128)} custom-call(s32[128]{0:T(128)} %desks.1, s32[128]{0:T(128)} %columns.1, s32[1]{0:T(128)S(6)} %copy.11.live, bf16[640,2048]{1,0:T(8,128)(2,1)} %hist_hbm.1, bf16[128,128,128]{2,1,0:T(8,128)(2,1)} %delta_hbm.1, bf16[128,128,128]{2,1,0:T(8,128)(2,1)} %gamma_hbm.1), custom_call_target="tpu_custom_call" | custom-call | tf_op jit(solution)/shard_map/block_products/pallas_call | solution.py:207
  7.9 34.1 %desk_exchange.1 = (f32[128,1024]{1,0:T(8,128)}, f32[1,1024]{1,0:T(1,128)}) custom-call(s32[1,1024]{1,0:T(1,128)} %bitcast.2, f32[9,128,640]{2,1,0:T(8,128)} %block_products.1.tiles), custom_call_target="tpu_custom_call" | custom-call | tf_op jit(solution)/shard_map/desk_exchange/pallas_call | solution.py:228
  42.0 1.9 %copy.12 = f32[128,1024]{1,0:T(8,128)} copy(f32[128,1024]{1,0:T(8,128)} %get-tuple-element.8) | data formatting | bytes 1048576
  43.9 1.3 %copy.13 = f32[1024]{0:T(1024)} copy(f32[1024]{0:T(1024)} %bitcast.3) | data formatting | bytes 8192
